TPU v7x, 32 devices: a whole 2x2x4 slice. The times are simulated.
32 devices in a mesh: dp: 8 (over z, y), head: 4 (over x, core).
Axes of the slice: x: 2, y: 2, z: 4, core: 2. Of those that a mesh axis runs over, the one named last changes fastest.
Arguments:
- qkv_raw: bfloat16 [8, 3, 512, 3072], P('dp', None, 'head'), may hold values from -6 to 6
- out_grad: bfloat16 [8, 512, 3072], P('dp', 'head')
- q_gain: float32 [128], replicated, may hold values from 0.25 to 1.75
- k_gain: float32 [128], replicated, may hold values from 0.25 to 1.75
- block_cols: int32 [24, 4, 4], replicated, may hold values from 0 to 3, as said below
- block_count: int32 [24, 4], replicated, may hold values from 1 to 4, as said below
Outputs:
- qkv_grad: bfloat16 [8, 3, 512, 3072], P('dp', None, 'head')
- attn_out: bfloat16 [8, 512, 3072], P('dp', 'head')
- gain_grad: float32 [2, 128], replicated
Inputs may be any that keep to these rules, and one draw needn't show every extreme that they name: `block_cols`: for every head and query block the 4 listed key blocks are distinct. `block_count`: some entry equals 4; heads differ in how many blocks they use.
All inputs are finite; a program needn't handle non-finite values.
Results may differ from a plain program's by a relative error of at most 0.008.
Values may be sent and summed in bfloat16 or wider, within the bound.
A program may use at most 64 MiB of HBM per device.

v0:
```python
import jax
import jax.numpy as jnp
from jax import lax
from jax.sharding import PartitionSpec as P

BLK = 128


def normalize(raw_rows, gain):
    widened = raw_rows.astype(jnp.float32)
    inverse = lax.rsqrt(jnp.mean(widened * widened, axis=-1, keepdims=True) + 1e-06)
    unit_rows = widened * inverse
    return (unit_rows, inverse, (unit_rows * gain).astype(jnp.bfloat16))


def norm_backward(grad_rows, unit_rows, inverse, gain):
    widened = grad_rows.astype(jnp.float32)
    scaled = widened * gain
    inner = jnp.mean(unit_rows * scaled, axis=-1, keepdims=True)
    grad_raw = (inverse * (scaled - unit_rows * inner)).astype(jnp.bfloat16)
    return (grad_raw, jnp.sum(widened * unit_rows, axis=(0, 1)))


def head_forward(queries, key_rows, value_rows, key_cols, counts):
    length, head_dim = queries.shape
    blocks = length // BLK
    score_scale = head_dim ** (-0.5)
    query_blocks = queries.reshape(blocks, BLK, head_dim)
    key_blocks = key_rows.reshape(blocks, BLK, head_dim)
    value_blocks = value_rows.reshape(blocks, BLK, head_dim)

    def advance(which, state):
        numer, totals = state
        column = lax.dynamic_index_in_dim(key_cols, which, 1, keepdims=False)
        is_live = (counts > which).astype(jnp.float32)
        key_block = jnp.take(key_blocks, column, axis=0)
        value_block = jnp.take(value_blocks, column, axis=0)
        scores = (
            jnp.einsum("qad,qbd->qab", query_blocks, key_block, preferred_element_type=jnp.float32)
            * score_scale
        )
        weights = jnp.exp(scores) * is_live[:, None, None]
        numer = numer + jnp.einsum(
            "qab,qbd->qad",
            weights.astype(jnp.bfloat16),
            value_block,
            preferred_element_type=jnp.float32,
        )
        return (numer, totals + jnp.sum(weights, axis=-1))

    start = (jnp.zeros((blocks, BLK, head_dim), jnp.float32), jnp.zeros((blocks, BLK), jnp.float32))
    numer, totals = lax.fori_loop(0, jnp.max(counts), advance, start)
    output = (numer / totals[:, :, None]).astype(jnp.bfloat16).reshape(length, head_dim)
    return (output, totals)


def head_backward(queries, key_rows, value_rows, grad_rows, output, totals, key_cols, counts):
    length, head_dim = queries.shape
    blocks = length // BLK
    score_scale = head_dim ** (-0.5)
    query_blocks = queries.reshape(blocks, BLK, head_dim)
    key_blocks = key_rows.reshape(blocks, BLK, head_dim)
    value_blocks = value_rows.reshape(blocks, BLK, head_dim)
    grad_blocks = grad_rows.reshape(blocks, BLK, head_dim)
    deltas = jnp.sum(output.astype(jnp.float32) * grad_rows.astype(jnp.float32), axis=-1).reshape(
        blocks, BLK
    )

    def advance(which, state):
        grad_query, grad_key, grad_value = state
        column = lax.dynamic_index_in_dim(key_cols, which, 1, keepdims=False)
        is_live = (counts > which).astype(jnp.float32)
        key_block = jnp.take(key_blocks, column, axis=0)
        value_block = jnp.take(value_blocks, column, axis=0)
        scores = (
            jnp.einsum("qad,qbd->qab", query_blocks, key_block, preferred_element_type=jnp.float32)
            * score_scale
        )
        probs = jnp.exp(scores) / totals[:, :, None] * is_live[:, None, None]
        grad_value = grad_value.at[column].add(
            jnp.einsum(
                "qab,qad->qbd",
                probs.astype(jnp.bfloat16),
                grad_blocks,
                preferred_element_type=jnp.float32,
            )
        )
        dprob = jnp.einsum(
            "qad,qbd->qab", grad_blocks, value_block, preferred_element_type=jnp.float32
        )
        dscore = (probs * (dprob - deltas[:, :, None])).astype(jnp.bfloat16)
        grad_query = (
            grad_query
            + jnp.einsum("qab,qbd->qad", dscore, key_block, preferred_element_type=jnp.float32)
            * score_scale
        )
        grad_key = grad_key.at[column].add(
            jnp.einsum("qab,qad->qbd", dscore, query_blocks, preferred_element_type=jnp.float32)
            * score_scale
        )
        return (grad_query, grad_key, grad_value)

    empty = jnp.zeros((blocks, BLK, head_dim), jnp.float32)
    grad_query, grad_key, grad_value = lax.fori_loop(
        0, jnp.max(counts), advance, (empty, empty, empty)
    )
    shape_back = (length, head_dim)
    return (
        grad_query.astype(jnp.bfloat16).reshape(shape_back),
        grad_key.astype(jnp.bfloat16).reshape(shape_back),
        grad_value.astype(jnp.bfloat16).reshape(shape_back),
    )


def body(qkv_raw, out_grad, q_gain, k_gain, block_cols, block_count):
    token_count = qkv_raw.shape[2]
    width = qkv_raw.shape[3]
    head_count = block_cols.shape[0]
    head_dim = width // head_count
    dev_count = lax.axis_size("head")
    my_index = lax.axis_index("head")
    raw_heads = qkv_raw[0].reshape(3, token_count, head_count, head_dim)
    unit_query, inv_query, norm_query = normalize(raw_heads[0], q_gain)
    unit_key, inv_key, norm_key = normalize(raw_heads[1], k_gain)
    value_heads = raw_heads[2]
    grad_heads = out_grad[0].reshape(token_count, head_count, head_dim)
    base_cap = -(-head_count // dev_count)
    owners = jnp.arange(head_count) // base_cap
    onehot = (owners[:, None] == jnp.arange(dev_count)[None, :]).astype(jnp.int32)
    earlier = jnp.cumsum(onehot, axis=0) - onehot
    send_rows = owners * base_cap + jnp.sum(earlier * onehot, axis=1)
    matches = (send_rows[None, :] == jnp.arange(dev_count * base_cap)[:, None]).astype(jnp.int32)
    head_of = jnp.sum(matches * jnp.arange(head_count)[None, :], axis=1)
    is_filled = jnp.sum(matches, axis=1) > 0

    def packed(rows_in):
        picked = jnp.take(rows_in, head_of, axis=1)
        return jnp.where(is_filled[None, :, None], picked, jnp.zeros((), rows_in.dtype))

    query_own, key_own, value_own, grad_own = (
        lax.all_to_all(packed(norm_query), "head", split_axis=1, concat_axis=0, tiled=True),
        lax.all_to_all(packed(norm_key), "head", split_axis=1, concat_axis=0, tiled=True),
        lax.all_to_all(packed(value_heads), "head", split_axis=1, concat_axis=0, tiled=True),
        lax.all_to_all(packed(grad_heads), "head", split_axis=1, concat_axis=0, tiled=True),
    )
    my_heads = lax.dynamic_slice_in_dim(head_of, my_index * base_cap, base_cap)
    my_filled = lax.dynamic_slice_in_dim(is_filled.astype(jnp.int32), my_index * base_cap, base_cap)
    owned = jnp.sum(my_filled)
    length = query_own.shape[0]
    blocks = length // BLK

    def forward_slot(slot, state):
        outputs, totals_all = state
        head = my_heads[slot]
        output, totals = head_forward(
            lax.dynamic_index_in_dim(query_own, slot, 1, keepdims=False),
            lax.dynamic_index_in_dim(key_own, slot, 1, keepdims=False),
            lax.dynamic_index_in_dim(value_own, slot, 1, keepdims=False),
            block_cols[head],
            block_count[head],
        )
        outputs = lax.dynamic_update_index_in_dim(outputs, output, slot, 1)
        return (outputs, lax.dynamic_update_index_in_dim(totals_all, totals, slot, 0))

    zero_rows = jnp.zeros((length, base_cap, head_dim), jnp.bfloat16)
    start = (zero_rows, jnp.ones((base_cap, blocks, BLK), jnp.float32))
    outputs, totals_all = lax.fori_loop(0, owned, forward_slot, start)

    def backward_slot(slot, state):
        grads_q, grads_k, grads_v = state
        head = my_heads[slot]
        grad_query, grad_key, grad_value = head_backward(
            lax.dynamic_index_in_dim(query_own, slot, 1, keepdims=False),
            lax.dynamic_index_in_dim(key_own, slot, 1, keepdims=False),
            lax.dynamic_index_in_dim(value_own, slot, 1, keepdims=False),
            lax.dynamic_index_in_dim(grad_own, slot, 1, keepdims=False),
            lax.dynamic_index_in_dim(outputs, slot, 1, keepdims=False),
            lax.dynamic_index_in_dim(totals_all, slot, 0, keepdims=False),
            block_cols[head],
            block_count[head],
        )
        return (
            lax.dynamic_update_index_in_dim(grads_q, grad_query, slot, 1),
            lax.dynamic_update_index_in_dim(grads_k, grad_key, slot, 1),
            lax.dynamic_update_index_in_dim(grads_v, grad_value, slot, 1),
        )

    grads_q, grads_k, grads_v = lax.fori_loop(
        0, owned, backward_slot, (zero_rows, zero_rows, zero_rows)
    )
    back_out, back_q, back_k, back_v = (
        lax.all_to_all(outputs, "head", split_axis=0, concat_axis=1, tiled=True),
        lax.all_to_all(grads_q, "head", split_axis=0, concat_axis=1, tiled=True),
        lax.all_to_all(grads_k, "head", split_axis=0, concat_axis=1, tiled=True),
        lax.all_to_all(grads_v, "head", split_axis=0, concat_axis=1, tiled=True),
    )
    out_heads = jnp.take(back_out, send_rows, axis=1)
    grad_query_heads = jnp.take(back_q, send_rows, axis=1)
    grad_key_heads = jnp.take(back_k, send_rows, axis=1)
    grad_value_heads = jnp.take(back_v, send_rows, axis=1)
    grad_raw_q, gain_q = norm_backward(grad_query_heads, unit_query, inv_query, q_gain)
    grad_raw_k, gain_k = norm_backward(grad_key_heads, unit_key, inv_key, k_gain)
    total_q, total_k = lax.psum((gain_q, gain_k), ("dp", "head"))
    clip_total = qkv_raw.shape[0] * lax.axis_size("dp")
    gain_grad = jnp.stack([total_q, total_k], axis=0) / clip_total
    qkv_grad = jnp.stack([grad_raw_q, grad_raw_k, grad_value_heads], axis=0).reshape(
        1, 3, token_count, width
    )
    attn_out = out_heads.reshape(1, token_count, width)
    return (qkv_grad, attn_out, gain_grad)


def solution(mesh):
    placed = (P("dp", None, "head", None), P("dp", "head", None), P(), P(), P(), P())
    return jax.shard_map(
        body,
        mesh=mesh,
        in_specs=placed,
        out_specs=(P("dp", None, "head", None), P("dp", "head", None), P()),
        check_vma=False,
    )
```

profile of v0, /device:TPU:0, one launch (start us, length us, event | category | flops | bytes accessed | tf_op | source)
XLA Modules:
  0.0 459.0 jit_solution(11162518513018739604)
XLA Ops:
  24.4 2.9 bitcast_select_fusion
  27.3 15.7 %all_to_all.144 = bf16[128,24,128]{2,0,1:T(8,128)(2,1)S(1)} all-to-all(bf16[128,24,128]{2,0,1:T(8,128)(2,1)S(1)} %get-tuple-element.620), channel_id=1, replica_groups=mesh['dp'=8,'head'=4] {'head'}, dimensions={1} | all-to-all | bytes 1572864 | tf_op jit(solution)/shard_map/all_to_all | solution.py:144
  43.0 14.8 %all_to_all.145 = bf16[128,24,128]{2,0,1:T(8,128)(2,1)} all-to-all(bf16[128,24,128]{2,0,1:T(8,128)(2,1)S(1)} %get-tuple-element.621), channel_id=1, replica_groups=mesh['dp'=8,'head'=4] {'head'}, dimensions={1} | all-to-all | bytes 1572864 | tf_op jit(solution)/shard_map/all_to_all | solution.py:143
  57.7 14.9 %all_to_all.146 = bf16[128,24,128]{2,0,1:T(8,128)(2,1)} all-to-all(bf16[128,24,128]{2,0,1:T(8,128)(2,1)S(1)} %get-tuple-element.622), channel_id=1, replica_groups=mesh['dp'=8,'head'=4] {'head'}, dimensions={1} | all-to-all | bytes 1572864 | tf_op jit(solution)/shard_map/all_to_all | solution.py:141
  72.6 3.5 all-to-all-start
  80.4 7.3 %all-to-all-done = bf16[128,24,128]{2,0,1:T(8,128)(2,1)S(1)} async-done(((bf16[128,24,128]{2,0,1:T(8,128)(2,1)}), bf16[128,24,128]{2,0,1:T(8,128)(2,1)S(1)}, u32[]{:S(2)}, u32[]{:S(2)}) %all-to-all-start) | async-done | bytes 786464 | tf_op jit(solution)/shard_map/all_to_all | solution.py:142
  89.7 78.7 %while.53 = (s32[]{:T(128)}, bf16[512,6,128]{2,0,1:T(8,128)(2,1)}, f32[6,4,128]{2,1,0:T(4,128)S(1)}, s32[]{:T(128)}, s32[6]{0:T(128)S(1)}, /*index=5*/s32[24,4]{...) while((s32[]{:T(128)}, bf16[512,6,128]{2,0,1:T(8,128)(2,1)}, ...), condition=%wide.region_12.15_spmd, body=%wide.region_7.0_spmd.sunk | while | flops 34145328 | bytes 3429340 | solution.py:167
  95.1 5.2 %while.56 = (s32[]{:T(128)}, f32[4,128,128]{2,1,0:T(8,128)S(1)}, f32[4,128]{1,0:T(4,128)S(1)}, s32[]{:T(128)}, s32[4,4]{0,1:T(4,128)S(1)}, /*index=5*/bf16[4,128...) while((s32[]{:T(128)}, f32[4,128,128]{2,1,0:T(8,128)S(1)}, ...), condition=%wide.region_11.13_spmd, body=%wide.region_9.12_spmd.sunk | while | flops 34014244 | bytes 1716531 | solution.py:52
  106.5 2.9 while.56
  115.7 7.5 %while.56 = (s32[]{:T(128)}, f32[4,128,128]{2,1,0:T(8,128)S(1)}, f32[4,128]{1,0:T(4,128)S(1)}, s32[]{:T(128)}, s32[4,4]{0,1:T(4,128)S(1)}, /*index=5*/bf16[4,128...) while((s32[]{:T(128)}, f32[4,128,128]{2,1,0:T(8,128)S(1)}, ...), condition=%wide.region_11.13_spmd, body=%wide.region_9.12_spmd.sunk | while | flops 34014244 | bytes 1716531 | solution.py:52
  129.5 9.9 %while.56 = (s32[]{:T(128)}, f32[4,128,128]{2,1,0:T(8,128)S(1)}, f32[4,128]{1,0:T(4,128)S(1)}, s32[]{:T(128)}, s32[4,4]{0,1:T(4,128)S(1)}, /*index=5*/bf16[4,128...) while((s32[]{:T(128)}, f32[4,128,128]{2,1,0:T(8,128)S(1)}, ...), condition=%wide.region_11.13_spmd, body=%wide.region_9.12_spmd.sunk | while | flops 34014244 | bytes 1716531 | solution.py:52
  145.6 9.9 %while.56 = (s32[]{:T(128)}, f32[4,128,128]{2,1,0:T(8,128)S(1)}, f32[4,128]{1,0:T(4,128)S(1)}, s32[]{:T(128)}, s32[4,4]{0,1:T(4,128)S(1)}, /*index=5*/bf16[4,128...) while((s32[]{:T(128)}, f32[4,128,128]{2,1,0:T(8,128)S(1)}, ...), condition=%wide.region_11.13_spmd, body=%wide.region_9.12_spmd.sunk | while | flops 34014244 | bytes 1716531 | solution.py:52
  161.7 5.2 %while.56 = (s32[]{:T(128)}, f32[4,128,128]{2,1,0:T(8,128)S(1)}, f32[4,128]{1,0:T(4,128)S(1)}, s32[]{:T(128)}, s32[4,4]{0,1:T(4,128)S(1)}, /*index=5*/bf16[4,128...) while((s32[]{:T(128)}, f32[4,128,128]{2,1,0:T(8,128)S(1)}, ...), condition=%wide.region_11.13_spmd, body=%wide.region_9.12_spmd.sunk | while | flops 34014244 | bytes 1716531 | solution.py:52
  171.3 137.9 %while.55 = (s32[]{:T(128)}, bf16[512,6,128]{2,0,1:T(8,128)(2,1)}, bf16[512,6,128]{2,0,1:T(8,128)(2,1)}, bf16[512,6,128]{2,0,1:T(8,128)(2,1)}, s32[]{:T(128)}, /...) while((s32[]{:T(128)}, bf16[512,6,128]{2,0,1:T(8,128)(2,1)}, ...), condition=%wide.region_20.23_spmd, body=%wide.region_13.22_spmd.sunk | while | flops 85328440 | bytes 9321624 | solution.py:188
  180.0 9.7 %while.57 = (s32[]{:T(128)}, f32[4,128,128]{2,1,0:T(8,128)S(1)}, f32[4,128,128]{2,1,0:T(8,128)S(1)}, f32[4,128,128]{2,1,0:T(8,128)S(1)}, s32[]{:T(128)}, /*index...) while((s32[]{:T(128)}, f32[4,128,128]{2,1,0:T(8,128)S(1)}, ...), condition=%wide.region_19.21_spmd, body=%wide.region_16.20_spmd.sunk | while | flops 84870192 | bytes 5251483 | solution.py:104
  199.9 5.2 %while.57 = (s32[]{:T(128)}, f32[4,128,128]{2,1,0:T(8,128)S(1)}, f32[4,128,128]{2,1,0:T(8,128)S(1)}, f32[4,128,128]{2,1,0:T(8,128)S(1)}, s32[]{:T(128)}, /*index...) while((s32[]{:T(128)}, f32[4,128,128]{2,1,0:T(8,128)S(1)}, ...), condition=%wide.region_19.21_spmd, body=%wide.region_16.20_spmd.sunk | while | flops 84870192 | bytes 5251483 | solution.py:104
  215.2 14.2 %while.57 = (s32[]{:T(128)}, f32[4,128,128]{2,1,0:T(8,128)S(1)}, f32[4,128,128]{2,1,0:T(8,128)S(1)}, f32[4,128,128]{2,1,0:T(8,128)S(1)}, s32[]{:T(128)}, /*index...) while((s32[]{:T(128)}, f32[4,128,128]{2,1,0:T(8,128)S(1)}, ...), condition=%wide.region_19.21_spmd, body=%wide.region_16.20_spmd.sunk | while | flops 84870192 | bytes 5251483 | solution.py:104
  239.6 18.8 %while.57 = (s32[]{:T(128)}, f32[4,128,128]{2,1,0:T(8,128)S(1)}, f32[4,128,128]{2,1,0:T(8,128)S(1)}, f32[4,128,128]{2,1,0:T(8,128)S(1)}, s32[]{:T(128)}, /*index...) while((s32[]{:T(128)}, f32[4,128,128]{2,1,0:T(8,128)S(1)}, ...), condition=%wide.region_19.21_spmd, body=%wide.region_16.20_spmd.sunk | while | flops 84870192 | bytes 5251483 | solution.py:104
  268.6 18.8 %while.57 = (s32[]{:T(128)}, f32[4,128,128]{2,1,0:T(8,128)S(1)}, f32[4,128,128]{2,1,0:T(8,128)S(1)}, f32[4,128,128]{2,1,0:T(8,128)S(1)}, s32[]{:T(128)}, /*index...) while((s32[]{:T(128)}, f32[4,128,128]{2,1,0:T(8,128)S(1)}, ...), condition=%wide.region_19.21_spmd, body=%wide.region_16.20_spmd.sunk | while | flops 84870192 | bytes 5251483 | solution.py:104
  297.5 9.7 %while.57 = (s32[]{:T(128)}, f32[4,128,128]{2,1,0:T(8,128)S(1)}, f32[4,128,128]{2,1,0:T(8,128)S(1)}, f32[4,128,128]{2,1,0:T(8,128)S(1)}, s32[]{:T(128)}, /*index...) while((s32[]{:T(128)}, f32[4,128,128]{2,1,0:T(8,128)S(1)}, ...), condition=%wide.region_19.21_spmd, body=%wide.region_16.20_spmd.sunk | while | flops 84870192 | bytes 5251483 | solution.py:104
  311.9 21.6 %all-to-all-start.6 = ((bf16[512,6,128]{2,1,0:T(8,128)(2,1)}), bf16[512,6,128]{2,1,0:T(8,128)(2,1)S(1)}, u32[]{:S(2)}, u32[]{:S(2)}) async-start(bf16[512,6,128]{2,1,0:T(8,128)(2,1)} %copy.125), calls=%async_computation.6 | async-start | bytes 2097152 | tf_op jit(solution)/shard_map/all_to_all | solution.py:195
  333.5 2.7 copy.117
  336.2 11.7 %all-to-all-done.6 = bf16[512,6,128]{2,1,0:T(8,128)(2,1)S(1)} async-done(((bf16[512,6,128]{2,1,0:T(8,128)(2,1)}), bf16[512,6,128]{2,1,0:T(8,128)(2,1)S(1)}, u32[]{:S(2)}, u32[]{:S(2)}) %all-to-all-start.6) | async-done | bytes 786464 | tf_op jit(solution)/shard_map/all_to_all | solution.py:195
  347.9 4.3 all-to-all-start.4
  353.7 13.0 %all-to-all-done.4 = bf16[512,6,128]{2,1,0:T(8,128)(2,1)} async-done(((bf16[512,6,128]{2,1,0:T(8,128)(2,1)}), bf16[512,6,128]{2,1,0:T(8,128)(2,1)}, u32[]{:S(2)}, u32[]{:S(2)}) %all-to-all-start.4) | async-done | bytes 786464 | tf_op jit(solution)/shard_map/all_to_all | solution.py:193
  366.7 4.4 all-to-all-start.5
  378.6 7.0 %all-to-all-done.5 = bf16[512,6,128]{2,1,0:T(8,128)(2,1)} async-done(((bf16[512,6,128]{2,1,0:T(8,128)(2,1)}), bf16[512,6,128]{2,1,0:T(8,128)(2,1)}, u32[]{:S(2)}, u32[]{:S(2)}) %all-to-all-start.5) | async-done | bytes 786464 | tf_op jit(solution)/shard_map/all_to_all | solution.py:194
  385.5 4.3 all-to-all-start.7
  392.2 2.7 gather_fusion.9
  394.9 3.5 fusion.43
  398.5 3.0 fusion.42
  417.5 41.0 %all-reduce = (f32[1,128]{1,0:T(1,128)S(1)}, f32[1,128]{1,0:T(1,128)S(1)}) all-reduce(f32[1,128]{1,0:T(1,128)S(1)} %bitcast.196, f32[1,128]{1,0:T(1,128)S(1)} %bitcast.195), channel_id=1, replica_groups=mesh['dp'=8,'head'=4] {'dp','head'}, use_global_device_ids=true, to_apply=%region_26.29 | all-reduce | flops 256 | bytes 2048 | tf_op jit(solution)/shard_map/psum | solution.py:203
  (572 shorter events, 222.0 us)
Async XLA Ops:
  8.0 7.9 %copy-start = (f32[128,24,128]{2,0,1:T(8,128)}, f32[128,24,128]{2,0,1:T(8,128)S(1)}, u32[]{:S(2)}) copy-start(f32[128,24,128]{2,0,1:T(8,128)S(1)} %copy.103) | copy-start | bytes 4718596
  10.9 5.0 %copy-start.13 = (f32[128]{0:T(128)S(1)}, f32[128]{0:T(128)}, u32[]{:S(2)}) copy-start(f32[128]{0:T(128)} %param.21) | copy-start | bytes 1540
  15.9 4.1 copy-start.12
  20.0 2.0 copy-start.4
  22.8 1.6 copy-start.9
  57.7 18.4 %copy-start.14 = (s32[24,4]{0,1:T(4,128)S(1)}, s32[24,4]{0,1:T(4,128)}, u32[]{:S(2)}) copy-start(s32[24,4]{0,1:T(4,128)} %param.23) | copy-start | bytes 1156
  57.7 19.2 %copy-start.11 = (s32[24,4,4]{0,2,1:T(4,128)S(1)}, s32[24,4,4]{0,2,1:T(4,128)}, u32[]{:S(2)}) copy-start(s32[24,4,4]{0,2,1:T(4,128)} %param.22) | copy-start | bytes 4612
  72.6 15.1 %all-to-all-start = ((bf16[128,24,128]{2,0,1:T(8,128)(2,1)}), bf16[128,24,128]{2,0,1:T(8,128)(2,1)S(1)}, u32[]{:S(2)}, u32[]{:S(2)}) async-start(bf16[128,24,128]{2,0,1:T(8,128)(2,1)} %get-tuple-element.623), calls=%async_computation | async-start | bytes 1572864 | tf_op jit(solution)/shard_map/all_to_all | solution.py:142
  77.1 1.4 copy-start.5
  77.1 2.4 copy-start.6
  311.9 36.0 %all-to-all-start.6 = ((bf16[512,6,128]{2,1,0:T(8,128)(2,1)}), bf16[512,6,128]{2,1,0:T(8,128)(2,1)S(1)}, u32[]{:S(2)}, u32[]{:S(2)}) async-start(bf16[512,6,128]{2,1,0:T(8,128)(2,1)} %copy.125), calls=%async_computation.6 | async-start | bytes 2097152 | tf_op jit(solution)/shard_map/all_to_all | solution.py:195
  333.5 18.7 %copy-start.7 = (bf16[512,6,128]{2,0,1:T(8,128)(2,1)S(1)}, bf16[512,6,128]{2,0,1:T(8,128)(2,1)}, u32[]{:S(2)}) copy-start(bf16[512,6,128]{2,0,1:T(8,128)(2,1)} %get-tuple-element.256) | copy-start | bytes 2359300
  347.9 18.8 %all-to-all-start.4 = ((bf16[512,6,128]{2,1,0:T(8,128)(2,1)}), bf16[512,6,128]{2,1,0:T(8,128)(2,1)}, u32[]{:S(2)}, u32[]{:S(2)}) async-start(bf16[512,6,128]{2,1,0:T(8,128)(2,1)} %copy.117), calls=%async_computation.4 | async-start | bytes 2097152 | tf_op jit(solution)/shard_map/all_to_all | solution.py:193
  366.7 18.8 %all-to-all-start.5 = ((bf16[512,6,128]{2,1,0:T(8,128)(2,1)}), bf16[512,6,128]{2,1,0:T(8,128)(2,1)}, u32[]{:S(2)}, u32[]{:S(2)}) async-start(bf16[512,6,128]{2,1,0:T(8,128)(2,1)} %copy.121), calls=%async_computation.5 | async-start | bytes 2097152 | tf_op jit(solution)/shard_map/all_to_all | solution.py:194
  385.5 18.8 %all-to-all-start.7 = ((bf16[512,6,128]{2,1,0:T(8,128)(2,1)}), bf16[512,6,128]{2,1,0:T(8,128)(2,1)}, u32[]{:S(2)}, u32[]{:S(2)}) async-start(bf16[512,6,128]{2,1,0:T(8,128)(2,1)} %copy.129), calls=%async_computation.7 | async-start | bytes 2097152 | tf_op jit(solution)/shard_map/all_to_all | solution.py:192
  389.8 5.1 %copy-start.1 = (f32[128,24,128]{2,0,1:T(8,128)S(1)}, f32[128,24,128]{2,0,1:T(8,128)}, u32[]{:S(2)}) copy-start(f32[128,24,128]{2,0,1:T(8,128)} %copy-done) | copy-start | bytes 4718596
  394.9 3.5 copy-start.2
  394.9 3.5 copy-start.3
  401.5 1.6 copy-start.10
  404.3 3.0 copy-start.8
where the time goes:
time: 455 us; the launch traced here: 459 us
  local copies, waits for them, and re-layouts  151 us (33%)
  blocking collectives  86.3 us (19%)
  other arithmetic  58.8 us (13%)
  loops' own time  57.9 us (13%)
  waiting for transfers between devices  39 us (9%)
  starting transfers between devices  38 us (8%)
  matrix products  27.1 us (6%)
    psum x1, blocking collectives, body(): total_q, total_k = lax.psum((gain_q, gain_k), ('dp', 'head'))  41 us
    all_to_all x1, starting transfers between devices, body(): lax.all_to_all(grads_v, 'head', split_axis=0, concat_axis=1, tiled=True)  21.6 us
    gather x32, local copies, waits for them, and re-layouts, advance(): value_block = jnp.take(value_blocks, column, axis=0)  18.3 us
    gather x32, local copies, waits for them, and re-layouts, advance(): key_block = jnp.take(key_blocks, column, axis=0)  18.3 us
    another operation x1, loops' own time, body(): lax.fori_loop(0, owned, backward_slot, (zero_rows, zero_rows, zero_rows))  15.7 us
    all_to_all x1, blocking collectives, body(): lax.all_to_all(packed(grad_heads), 'head', split_axis=1, concat_axis=0, t...  15.7 us
    another operation x6, loops' own time, head_backward(): lax.fori_loop(0, jnp.max(counts), advance, (empty, empty, empty))  15.4 us
    all_to_all x1, blocking collectives, body(): lax.all_to_all(packed(norm_query), 'head', split_axis=1, concat_axis=0, t...  14.9 us
  transfers between devices with their start and end apart: 5, of which 4 were waited for; matrix products, arithmetic and copies ran while one was open for 7% of the time, Pallas kernels for 0%

commit v1 on v0

v1 whole, which is shorter than its diff:
```python
import functools

import jax
import jax.numpy as jnp
from jax import lax
from jax.experimental import pallas as pl
from jax.experimental.pallas import tpu as pltpu
from jax.sharding import PartitionSpec as P

BLK = 128
MESH = pl.DeviceIdType.MESH
NT = (((1,), (1,)), ((), ()))
TN = (((0,), (0,)), ((), ()))


def dot_f32(left, right, dims=(((1,), (0,)), ((), ()))):
    return lax.dot_general(left, right, dims, preferred_element_type=jnp.float32)


def normalize(raw_rows, gain):
    widened = raw_rows.astype(jnp.float32)
    inverse = lax.rsqrt(jnp.mean(widened * widened, axis=-1, keepdims=True) + 1e-06)
    unit_rows = widened * inverse
    return unit_rows, inverse, (unit_rows * gain).astype(jnp.bfloat16)


def norm_backward(grad_rows, unit_rows, inverse, gain):
    widened = grad_rows.astype(jnp.float32)
    scaled = widened * gain
    inner = jnp.mean(unit_rows * scaled, axis=-1, keepdims=True)
    grad_raw = (inverse * (scaled - unit_rows * inner)).astype(jnp.bfloat16)
    return grad_raw, jnp.sum(widened * unit_rows, axis=0, keepdims=True)


def kernel(
    n, dp, slots, clips,
    qkv_hbm, grad_hbm, gains_ref, live_ref,
    dqkv_hbm, out_hbm, gain_out,
    raw_buf, grad_buf, res_buf, res_out, norm_buf, prob_buf, ds_buf, sums, part_dp, part_head,
    fwd_send, fwd_recv, own_sem, back_send, back_recv, own_back, red_send, red_recv,
):
    me = lax.axis_index("head")
    my_dp = lax.axis_index("dp")
    tokens = BLK
    length = n * tokens
    head_dim = raw_buf.shape[-1]
    scale = head_dim ** (-0.5)

    def rows(index):
        return pl.ds(pl.multiple_of(index * tokens, tokens), tokens)

    def cols(head):
        return pl.ds(pl.multiple_of(head * head_dim, head_dim), head_dim)

    def forward_copies(slot, step, source):
        target = lax.rem(me + step, n)
        head = target * slots + slot
        return (
            pltpu.make_async_remote_copy(
                src_ref=qkv_hbm.at[:, :, cols(head)],
                dst_ref=raw_buf.at[slot, :, rows(source), :],
                send_sem=fwd_send.at[slot, step, 0],
                recv_sem=fwd_recv.at[slot, step, 0],
                device_id={"head": target},
                device_id_type=MESH,
            ),
            pltpu.make_async_remote_copy(
                src_ref=grad_hbm.at[:, cols(head)],
                dst_ref=grad_buf.at[slot, rows(source), :],
                send_sem=fwd_send.at[slot, step, 1],
                recv_sem=fwd_recv.at[slot, step, 1],
                device_id={"head": target},
                device_id_type=MESH,
            ),
        )

    def own_copies(slot):
        head = me * slots + slot
        return (
            pltpu.make_async_copy(
                qkv_hbm.at[:, :, cols(head)], raw_buf.at[slot, :, rows(me), :], own_sem.at[slot, 0]
            ),
            pltpu.make_async_copy(
                grad_hbm.at[:, cols(head)], grad_buf.at[slot, rows(me), :], own_sem.at[slot, 1]
            ),
        )

    def back_copies(slot, step, owner):
        target = lax.rem(me + step, n)
        head = owner * slots + slot
        return (
            pltpu.make_async_remote_copy(
                src_ref=res_buf.at[slot, :, rows(target), :],
                dst_ref=dqkv_hbm.at[:, :, cols(head)],
                send_sem=back_send.at[slot, step, 0],
                recv_sem=back_recv.at[slot, step, 0],
                device_id={"head": target},
                device_id_type=MESH,
            ),
            pltpu.make_async_remote_copy(
                src_ref=res_out.at[slot, rows(target), :],
                dst_ref=out_hbm.at[:, cols(head)],
                send_sem=back_send.at[slot, step, 1],
                recv_sem=back_recv.at[slot, step, 1],
                device_id={"head": target},
                device_id_type=MESH,
            ),
        )

    def own_back_copies(slot):
        head = me * slots + slot
        return (
            pltpu.make_async_copy(
                res_buf.at[slot, :, rows(me), :], dqkv_hbm.at[:, :, cols(head)], own_back.at[slot, 0]
            ),
            pltpu.make_async_copy(
                res_out.at[slot, rows(me), :], out_hbm.at[:, cols(head)], own_back.at[slot, 1]
            ),
        )

    barrier = pltpu.get_barrier_semaphore()
    for step in range(1, n):
        pl.semaphore_signal(
            barrier, inc=1, device_id={"head": lax.rem(me + step, n)}, device_id_type=MESH
        )
    for step in range(1, dp):
        pl.semaphore_signal(
            barrier, inc=1, device_id={"dp": lax.rem(my_dp + step, dp)}, device_id_type=MESH
        )
    pl.semaphore_wait(barrier, n - 1 + dp - 1)

    @pl.loop(0, slots)
    def _(slot):
        for step in range(1, n):
            for copy in forward_copies(slot, step, me):
                copy.start()
        for copy in own_copies(slot):
            copy.start()

    sums[...] = jnp.zeros_like(sums)
    q_gain = gains_ref[0:1, :]
    k_gain = gains_ref[1:2, :]

    @pl.loop(0, slots)
    def _(slot):
        for copy in own_copies(slot):
            copy.wait()
        for step in range(1, n):
            for copy in forward_copies(slot, step, lax.rem(me + n - step, n)):
                copy.wait_recv()
        head = me * slots + slot
        norm_buf[0] = normalize(raw_buf[slot, 0], q_gain)[2]
        norm_buf[1] = normalize(raw_buf[slot, 1], k_gain)[2]
        for block in range(n):
            here = slice(block * tokens, (block + 1) * tokens)
            query = norm_buf[0, here]
            grads = grad_buf[slot, here]
            scores = dot_f32(query, norm_buf[1], NT) * scale
            weights = jnp.exp(scores) * live_ref[head, block : block + 1, :]
            total = jnp.sum(weights, axis=-1, keepdims=True)
            inverse = 1.0 / total
            numer = dot_f32(weights.astype(jnp.bfloat16), raw_buf[slot, 2])
            output = (numer * inverse).astype(jnp.bfloat16)
            res_out[slot, here] = output
            delta = jnp.sum(
                output.astype(jnp.float32) * grads.astype(jnp.float32), axis=-1, keepdims=True
            )
            probs = weights * inverse
            prob_buf[here] = probs.astype(jnp.bfloat16)
            dprob = dot_f32(grads, raw_buf[slot, 2], NT)
            dscore = (probs * (dprob - delta)).astype(jnp.bfloat16)
            ds_buf[here] = dscore
            grad_query = (dot_f32(dscore, norm_buf[1]) * scale).astype(jnp.bfloat16)
            unit, inv, _ = normalize(raw_buf[slot, 0, here], q_gain)
            raw_grad, gain_part = norm_backward(grad_query, unit, inv, q_gain)
            res_buf[slot, 0, here] = raw_grad
            sums[0:1] += gain_part
        for block in range(n):
            here = slice(block * tokens, (block + 1) * tokens)
            res_buf[slot, 2, here] = dot_f32(prob_buf[:, here], grad_buf[slot], TN).astype(
                jnp.bfloat16
            )
            grad_key = (dot_f32(ds_buf[:, here], norm_buf[0], TN) * scale).astype(jnp.bfloat16)
            unit, inv, _ = normalize(raw_buf[slot, 1, here], k_gain)
            raw_grad, gain_part = norm_backward(grad_key, unit, inv, k_gain)
            res_buf[slot, 1, here] = raw_grad
            sums[1:2] += gain_part
        for step in range(1, n):
            for copy in back_copies(slot, step, me):
                copy.start()
        for copy in own_back_copies(slot):
            copy.start()

    def reduce_copy(axis, part, step, place, base, size):
        position = my_dp if axis == "dp" else me
        return pltpu.make_async_remote_copy(
            src_ref=sums,
            dst_ref=part.at[place],
            send_sem=red_send.at[base + step],
            recv_sem=red_recv.at[base + step],
            device_id={axis: lax.rem(position + step, size)},
            device_id_type=MESH,
        )

    def reduce_stage(axis, part, position, base, size):
        for step in range(1, size):
            reduce_copy(axis, part, step, position, base, size).start()
        part[position] = sums[...]
        for step in range(1, size):
            copy = reduce_copy(axis, part, step, lax.rem(position + size - step, size), base, size)
            copy.wait_recv()
        for step in range(1, size):
            reduce_copy(axis, part, step, position, base, size).wait_send()
        total = part[0]
        for index in range(1, size):
            total = total + part[index]
        sums[...] = total

    reduce_stage("dp", part_dp, my_dp, 0, dp)
    reduce_stage("head", part_head, me, dp, n)
    gain_out[...] = sums[0:2, :] * (1.0 / clips)

    @pl.loop(0, slots)
    def _(slot):
        for step in range(1, n):
            for copy in forward_copies(slot, step, me):
                copy.wait_send()
            for copy in back_copies(slot, step, me):
                copy.wait_send()
            for copy in back_copies(slot, step, lax.rem(me + n - step, n)):
                copy.wait_recv()
        for copy in own_back_copies(slot):
            copy.wait()


def body(qkv_raw, out_grad, q_gain, k_gain, block_cols, block_count):
    _, _, tokens, width = qkv_raw.shape
    heads, blocks, listed = block_cols.shape
    head_dim = width // heads
    n = lax.axis_size("head")
    dp = lax.axis_size("dp")
    slots = heads // n
    length = n * tokens
    clips = qkv_raw.shape[0] * dp
    used = jnp.arange(listed)[None, None, :] < block_count[:, :, None]
    key_block = jnp.arange(length) // BLK
    live = jnp.any(
        (block_cols[:, :, :, None] == key_block[None, None, None, :]) & used[:, :, :, None], axis=2
    ).astype(jnp.float32)
    gains = jnp.stack([q_gain, k_gain], axis=0)
    dma = pltpu.SemaphoreType.DMA
    vmem = pl.BlockSpec(memory_space=pltpu.VMEM)
    hbm = pl.BlockSpec(memory_space=pl.ANY)
    qkv_grad, attn_out, gain_grad = pl.pallas_call(
        functools.partial(kernel, n, dp, slots, clips),
        out_shape=(
            jax.ShapeDtypeStruct((3, tokens, width), jnp.bfloat16),
            jax.ShapeDtypeStruct((tokens, width), jnp.bfloat16),
            jax.ShapeDtypeStruct((2, head_dim), jnp.float32),
        ),
        in_specs=[hbm, hbm, vmem, vmem],
        out_specs=(hbm, hbm, vmem),
        scratch_shapes=[
            pltpu.VMEM((slots, 3, length, head_dim), jnp.bfloat16),
            pltpu.VMEM((slots, length, head_dim), jnp.bfloat16),
            pltpu.VMEM((slots, 3, length, head_dim), jnp.bfloat16),
            pltpu.VMEM((slots, length, head_dim), jnp.bfloat16),
            pltpu.VMEM((2, length, head_dim), jnp.bfloat16),
            pltpu.VMEM((length, length), jnp.bfloat16),
            pltpu.VMEM((length, length), jnp.bfloat16),
            pltpu.VMEM((8, head_dim), jnp.float32),
            pltpu.VMEM((dp, 8, head_dim), jnp.float32),
            pltpu.VMEM((n, 8, head_dim), jnp.float32),
            dma((slots, n, 2)),
            dma((slots, n, 2)),
            dma((slots, 2)),
            dma((slots, n, 2)),
            dma((slots, n, 2)),
            dma((slots, 2)),
            dma((dp + n,)),
            dma((dp + n,)),
        ],
        compiler_params=pltpu.CompilerParams(
            collective_id=0, has_side_effects=True, vmem_limit_bytes=40 * 2**20
        ),
        cost_estimate=pl.CostEstimate(
            flops=14 * slots * length * length * head_dim,
            bytes_accessed=16 * tokens * width,
            transcendentals=slots * length * length,
        ),
    )(qkv_raw[0], out_grad[0], gains, live)
    return qkv_grad[None], attn_out[None], gain_grad


def solution(mesh):
    placed = (P("dp", None, "head", None), P("dp", "head", None), P(), P(), P(), P())
    return jax.shard_map(
        body,
        mesh=mesh,
        in_specs=placed,
        out_specs=(P("dp", None, "head", None), P("dp", "head", None), P()),
        check_vma=False,
    )
```

time: 455 us -> 86.8 us (0.19)
  local copies, waits for them, and re-layouts: 151 us -> 5.77 us
  blocking collectives: 86.3 us -> 0 us
  Pallas kernels: 0 us -> 77.8 us
  loops' own time: 57.9 us -> 0 us
  other arithmetic: 58.8 us -> 2.27 us
  waiting for transfers between devices: 39 us -> 0 us
  starting transfers between devices: 38 us -> 0 us
  matrix products: 27.1 us -> 0 us
    pallas_call x0 -> x1, Pallas kernels: none -> 77.8 us  [body(): pl.pallas_call(functools.partial(kernel, n, dp, slots, clips), out_shape=...]
    another operation x14 -> x0, loops' own time: 57.9 us -> none  [the longest x1 15.7 us: body(): lax.fori_loop(0, owned, backward_slot, (zero_rows, zero_rows, zero_rows))]
    gather x72 -> x0, local copies, waits for them, and re-layouts: 52.5 us -> none  [the longest x32 18.3 us: advance(): value_block = jnp.take(value_blocks, column, axis=0)]
    all_to_all x3 -> x0, blocking collectives: 45.3 us -> none  [the longest x1 15.7 us: body(): lax.all_to_all(packed(grad_heads), 'head', split_axis=1, concat_axis=0, t...]
    psum x1 -> x0, blocking collectives: 41 us -> none  [body(): total_q, total_k = lax.psum((gain_q, gain_k), ('dp', 'head'))]
    dynamic_slice x49 -> x0, local copies, waits for them, and re-layouts: 40.5 us -> none  [the longest x6 5.96 us: forward_slot(): lax.dynamic_index_in_dim(value_own, slot, 1, keepdims=False)]
    all_to_all x5 -> x0, waiting for transfers between devices: 39 us -> none  [the longest x1 13 us: body(): lax.all_to_all(grads_q, 'head', split_axis=0, concat_axis=1, tiled=True)]
    all_to_all x5 -> x0, starting transfers between devices: 38 us -> none  [the longest x1 21.6 us: body(): lax.all_to_all(grads_v, 'head', split_axis=0, concat_axis=1, tiled=True)]
  transfers between devices with their start and end apart: 5 -> 0, of which waited for: 4 -> 0; matrix products, arithmetic and copies ran while one was open for 7% -> 0% of each run, Pallas kernels for 0% -> 0%
where the time goes in v1:
time: 86.8 us; the launch traced here: 86.5 us
  Pallas kernels  77.8 us (90%)
  local copies, waits for them, and re-layouts  5.77 us (7%)
  other arithmetic  2.27 us (3%)
    pallas_call x1, Pallas kernels, body(): pl.pallas_call(functools.partial(kernel, n, dp, slots, clips), out_shape=...  77.8 us
    unnamed x7, local copies, waits for them, and re-layouts  5.64 us

profile of v1, /device:TPU:0, one launch (start us, length us, event | category | flops | bytes accessed | tf_op | source)
XLA Modules:
  0.0 86.5 jit_solution(11721585547001430443)
XLA Ops:
  0.6 0.7 pad_maximum_fusion.gains_ref
  1.3 0.7 iota_compare_fusion
  2.0 0.9 %and_reduce_fusion = pred[24,4,512]{2,0,1:T(8,128)(4,1)S(1)} fusion(s32[512]{0:T(512)S(1)} %add_select_fusion, s32[24,4,4]{0,2,1:T(4,128)} %param.10, pred[24,4,4]{0,2,1:T(4,128)(4,1)S(1)} %iota_compare_fusion), kind=kLoop, calls=%fused_computation | loop fusion | flops 540672 | bytes 53120 | tf_op jit(solution)/shard_map/reduce_or | solution.py:247
  2.9 0.1 copy.12.live_ref
  3.1 0.0 copy-start
  3.1 1.7 %copy-done = bf16[1,3,128,3072]{3,2,1,0:T(8,128)(2,1)S(1)} copy-done((bf16[1,3,128,3072]{3,2,1,0:T(8,128)(2,1)S(1)}, bf16[1,3,128,3072]{3,2,1,0:T(8,128)(2,1)}, u32[]{:S(2)}) %copy-start) | copy-done | bytes 2359320
  4.7 0.0 copy-start.1
  4.7 1.1 %copy-done.1 = bf16[1,128,3072]{2,1,0:T(8,128)(2,1)S(1)} copy-done((bf16[1,128,3072]{2,1,0:T(8,128)(2,1)S(1)}, bf16[1,128,3072]{2,1,0:T(8,128)(2,1)}, u32[]{:S(2)}) %copy-start.1) | copy-done | bytes 786456
  5.9 77.8 %shard_map.85 = (bf16[3,128,3072]{2,1,0:T(8,128)(2,1)S(1)}, bf16[128,3072]{1,0:T(8,128)(2,1)S(1)}, f32[2,128]{1,0:T(2,128)S(1)}) custom-call(bf16[3,128,3072]{2,1,0:T(8,128)(2,1)S(1)} %bitcast.8, bf16[128,3072]{1,0:T(8,128)(2,1)S(1)} %bitcast.9, f32[2,128]{1,0:T(2,128)S(1)} %pad_maximum_fusion.gains_ref, f32[24,4,512]{2,1,0:T(4,128)S(1)} %copy.12.live_ref), custom_call_target="tpu_custom_call" | custom-call | flops 2818572288 | bytes 6291456 | tf_op jit(solution)/shard_map/pallas_call | solution.py:254
  83.7 1.4 %copy.16 = bf16[1,3,128,3072]{3,2,1,0:T(8,128)(2,1)} copy(bf16[1,3,128,3072]{3,2,1,0:T(8,128)(2,1)S(1)} %bitcast.6) | data formatting | bytes 4718592
  85.1 0.9 %copy.17 = bf16[1,128,3072]{2,1,0:T(8,128)(2,1)} copy(bf16[1,128,3072]{2,1,0:T(8,128)(2,1)S(1)} %bitcast.7) | data formatting | bytes 1572864
  85.9 0.6 copy.18
  (2 shorter events, 0.0 us)
Async XLA Ops:
  3.1 1.7 %copy-start = (bf16[1,3,128,3072]{3,2,1,0:T(8,128)(2,1)S(1)}, bf16[1,3,128,3072]{3,2,1,0:T(8,128)(2,1)}, u32[]{:S(2)}) copy-start(bf16[1,3,128,3072]{3,2,1,0:T(8,128)(2,1)} %param.6) | copy-start | bytes 7077892
  4.7 1.1 %copy-start.1 = (bf16[1,128,3072]{2,1,0:T(8,128)(2,1)S(1)}, bf16[1,128,3072]{2,1,0:T(8,128)(2,1)}, u32[]{:S(2)}) copy-start(bf16[1,128,3072]{2,1,0:T(8,128)(2,1)} %param.7) | copy-start | bytes 2359300

commit v2 on v1

--- a/solution.py
+++ b/solution.py
@@ -32,12 +32,29 @@
     return grad_raw, jnp.sum(widened * unit_rows, axis=0, keepdims=True)
 
 
+def pick_lane(values, head):
+    lanes = lax.broadcasted_iota(jnp.int32, values.shape, values.ndim - 1)
+    chosen = jnp.where(lanes == head, values.astype(jnp.float32), 0.0)
+    return jnp.sum(chosen, axis=-1, keepdims=True)
+
+
+def live_keys(counts, columns, block, length):
+    key_block = (lax.broadcasted_iota(jnp.int32, (1, length), 1) // BLK).astype(jnp.float32)
+    live = jnp.zeros((1, length), jnp.float32)
+    for which in range(columns.shape[1]):
+        used = counts[block : block + 1] > which
+        wanted = jnp.where(used, columns[block, which : which + 1], -1.0)
+        live = live + jnp.where(key_block == wanted, 1.0, 0.0)
+    return live
+
+
 def kernel(
     n, dp, slots, clips,
-    qkv_hbm, grad_hbm, gains_ref, live_ref,
+    qkv_hbm, grad_hbm, q_gain_hbm, k_gain_hbm, cols_hbm, count_hbm,
     dqkv_hbm, out_hbm, gain_out,
     raw_buf, grad_buf, res_buf, res_out, norm_buf, prob_buf, ds_buf, sums, part_dp, part_head,
-    fwd_send, fwd_recv, own_sem, back_send, back_recv, own_back, red_send, red_recv,
+    q_gain_ref, k_gain_ref, cols_ref, count_ref,
+    fwd_send, fwd_recv, own_sem, back_send, back_recv, own_back, red_send, red_recv, small_sem,
 ):
     me = lax.axis_index("head")
     my_dp = lax.axis_index("dp")
@@ -138,8 +155,23 @@
             copy.start()
 
     sums[...] = jnp.zeros_like(sums)
-    q_gain = gains_ref[0:1, :]
-    k_gain = gains_ref[1:2, :]
+    small_copies = [
+        pltpu.make_async_copy(source, target, small_sem.at[index])
+        for index, (source, target) in enumerate(
+            (
+                (q_gain_hbm, q_gain_ref),
+                (k_gain_hbm, k_gain_ref),
+                (cols_hbm, cols_ref),
+                (count_hbm, count_ref),
+            )
+        )
+    ]
+    for copy in small_copies:
+        copy.start()
+    for copy in small_copies:
+        copy.wait()
+    q_gain = q_gain_ref[...]
+    k_gain = k_gain_ref[...]
 
     @pl.loop(0, slots)
     def _(slot):
@@ -149,6 +181,8 @@
             for copy in forward_copies(slot, step, lax.rem(me + n - step, n)):
                 copy.wait_recv()
         head = me * slots + slot
+        counts = pick_lane(count_ref[...], head)
+        columns = pick_lane(cols_ref[...], head)
         norm_buf[0] = normalize(raw_buf[slot, 0], q_gain)[2]
         norm_buf[1] = normalize(raw_buf[slot, 1], k_gain)[2]
         for block in range(n):
@@ -156,7 +190,7 @@
             query = norm_buf[0, here]
             grads = grad_buf[slot, here]
             scores = dot_f32(query, norm_buf[1], NT) * scale
-            weights = jnp.exp(scores) * live_ref[head, block : block + 1, :]
+            weights = jnp.exp(scores) * live_keys(counts, columns, block, length)
             total = jnp.sum(weights, axis=-1, keepdims=True)
             inverse = 1.0 / total
             numer = dot_f32(weights.astype(jnp.bfloat16), raw_buf[slot, 2])
@@ -242,15 +276,10 @@
     slots = heads // n
     length = n * tokens
     clips = qkv_raw.shape[0] * dp
-    used = jnp.arange(listed)[None, None, :] < block_count[:, :, None]
-    key_block = jnp.arange(length) // BLK
-    live = jnp.any(
-        (block_cols[:, :, :, None] == key_block[None, None, None, :]) & used[:, :, :, None], axis=2
-    ).astype(jnp.float32)
-    gains = jnp.stack([q_gain, k_gain], axis=0)
     dma = pltpu.SemaphoreType.DMA
     vmem = pl.BlockSpec(memory_space=pltpu.VMEM)
-    hbm = pl.BlockSpec(memory_space=pl.ANY)
+    hbm = pl.BlockSpec(memory_space=pltpu.HBM)
+    anywhere = pl.BlockSpec(memory_space=pl.ANY)
     qkv_grad, attn_out, gain_grad = pl.pallas_call(
         functools.partial(kernel, n, dp, slots, clips),
         out_shape=(
@@ -258,8 +287,8 @@
             jax.ShapeDtypeStruct((tokens, width), jnp.bfloat16),
             jax.ShapeDtypeStruct((2, head_dim), jnp.float32),
         ),
-        in_specs=[hbm, hbm, vmem, vmem],
-        out_specs=(hbm, hbm, vmem),
+        in_specs=[hbm] * 6,
+        out_specs=(anywhere, anywhere, vmem),
         scratch_shapes=[
             pltpu.VMEM((slots, 3, length, head_dim), jnp.bfloat16),
             pltpu.VMEM((slots, length, head_dim), jnp.bfloat16),
@@ -271,6 +300,10 @@
             pltpu.VMEM((8, head_dim), jnp.float32),
             pltpu.VMEM((dp, 8, head_dim), jnp.float32),
             pltpu.VMEM((n, 8, head_dim), jnp.float32),
+            pltpu.VMEM((1, head_dim), jnp.float32),
+            pltpu.VMEM((1, head_dim), jnp.float32),
+            pltpu.VMEM((blocks, listed, heads), jnp.int32),
+            pltpu.VMEM((blocks, heads), jnp.int32),
             dma((slots, n, 2)),
             dma((slots, n, 2)),
             dma((slots, 2)),
@@ -279,16 +312,29 @@
             dma((slots, 2)),
             dma((dp + n,)),
             dma((dp + n,)),
+            dma((4,)),
         ],
         compiler_params=pltpu.CompilerParams(
-            collective_id=0, has_side_effects=True, vmem_limit_bytes=40 * 2**20
+            collective_id=0, has_side_effects=True, vmem_limit_bytes=50 * 2**20
         ),
         cost_estimate=pl.CostEstimate(
             flops=14 * slots * length * length * head_dim,
             bytes_accessed=16 * tokens * width,
             transcendentals=slots * length * length,
         ),
-    )(qkv_raw[0], out_grad[0], gains, live)
+    )(
+        *(
+            pltpu.with_memory_space_constraint(operand, pltpu.HBM)
+            for operand in (
+                qkv_raw[0],
+                out_grad[0],
+                q_gain.reshape(1, head_dim),
+                k_gain.reshape(1, head_dim),
+                jnp.transpose(block_cols, (1, 2, 0)),
+                block_count.T,
+            )
+        )
+    )
     return qkv_grad[None], attn_out[None], gain_grad
 
 

time: 86.8 us -> 81.7 us (0.941)
  local copies, waits for them, and re-layouts: 5.77 us -> 2.85 us
  other arithmetic: 2.27 us -> 0 us
    unnamed x7 -> x3, local copies, waits for them, and re-layouts: 5.64 us -> 2.85 us
    reduce_or x1 -> x0, other arithmetic: 0.88 us -> none  [body(): jnp.any((block_cols[:, :, :, None] == key_block[None, None, None, :]) & u...]
where the time goes in v2:
time: 81.7 us; the launch traced here: 81.6 us
  Pallas kernels  78.1 us (96%)
  local copies, waits for them, and re-layouts  2.85 us (3%)
    pallas_call x1, Pallas kernels, body(): pl.pallas_call(functools.partial(kernel, n, dp, slots, clips), out_shape=...  78.1 us
    unnamed x3, local copies, waits for them, and re-layouts  2.85 us

profile of v2, /device:TPU:0, one launch (start us, length us, event | category | flops | bytes accessed | tf_op | source)
XLA Modules:
  0.0 81.6 jit_solution(17248321420032603272)
XLA Ops:
  0.6 78.1 %shard_map.85 = (bf16[3,128,3072]{2,1,0:T(8,128)(2,1)S(1)}, bf16[128,3072]{1,0:T(8,128)(2,1)S(1)}, f32[2,128]{1,0:T(2,128)S(1)}) custom-call(bf16[3,128,3072]{2,1,0:T(8,128)(2,1)} %bitcast.10, bf16[128,3072]{1,0:T(8,128)(2,1)} %bitcast.11, f32[1,128]{1,0:T(1,128)} %bitcast.14, f32[1,128]{1,0:T(1,128)} %bitcast.15, s32[4,4,24]{2,1,0:T(4,128)} %bitcast.12, ...), custom_call_target="tpu_custom_call" | custom-call | flops 2818572288 | bytes 6291456 | tf_op jit(solution)/shard_map/pallas_call | solution.py:283
  78.7 1.4 %copy.12 = bf16[1,3,128,3072]{3,2,1,0:T(8,128)(2,1)} copy(bf16[1,3,128,3072]{3,2,1,0:T(8,128)(2,1)S(1)} %bitcast.8) | data formatting | bytes 4718592
  80.1 0.9 %copy.13 = bf16[1,128,3072]{2,1,0:T(8,128)(2,1)} copy(bf16[1,128,3072]{2,1,0:T(8,128)(2,1)S(1)} %bitcast.9) | data formatting | bytes 1572864
  81.0 0.6 copy.14

commit v3 on v2

--- a/solution.py
+++ b/solution.py
@@ -46,6 +46,10 @@
         wanted = jnp.where(used, columns[block, which : which + 1], -1.0)
         live = live + jnp.where(key_block == wanted, 1.0, 0.0)
     return live
+
+
+def partner(index, bit):
+    return index + bit - 2 * bit * lax.rem(index // bit, 2)
 
 
 def kernel(
@@ -140,11 +144,12 @@
         pl.semaphore_signal(
             barrier, inc=1, device_id={"head": lax.rem(me + step, n)}, device_id_type=MESH
         )
-    for step in range(1, dp):
+    bits = [1 << power for power in range(dp.bit_length() - 1)]
+    for bit in bits:
         pl.semaphore_signal(
-            barrier, inc=1, device_id={"dp": lax.rem(my_dp + step, dp)}, device_id_type=MESH
-        )
-    pl.semaphore_wait(barrier, n - 1 + dp - 1)
+            barrier, inc=1, device_id={"dp": partner(my_dp, bit)}, device_id_type=MESH
+        )
+    pl.semaphore_wait(barrier, n - 1 + len(bits))
 
     @pl.loop(0, slots)
     def _(slot):
@@ -226,13 +231,12 @@
             copy.start()
 
     def reduce_copy(axis, part, step, place, base, size):
-        position = my_dp if axis == "dp" else me
         return pltpu.make_async_remote_copy(
             src_ref=sums,
             dst_ref=part.at[place],
             send_sem=red_send.at[base + step],
             recv_sem=red_recv.at[base + step],
-            device_id={axis: lax.rem(position + step, size)},
+            device_id={axis: lax.rem(me + step, size)},
             device_id_type=MESH,
         )
 
@@ -250,7 +254,18 @@
             total = total + part[index]
         sums[...] = total
 
-    reduce_stage("dp", part_dp, my_dp, 0, dp)
+    for stage, bit in enumerate(bits):
+        copy = pltpu.make_async_remote_copy(
+            src_ref=sums,
+            dst_ref=part_dp.at[stage],
+            send_sem=red_send.at[stage],
+            recv_sem=red_recv.at[stage],
+            device_id={"dp": partner(my_dp, bit)},
+            device_id_type=MESH,
+        )
+        copy.start()
+        copy.wait()
+        sums[...] += part_dp[stage]
     reduce_stage("head", part_head, me, dp, n)
     gain_out[...] = sums[0:2, :] * (1.0 / clips)
 

time: 81.7 us -> 79.8 us (0.977)
  Pallas kernels: 78.1 us -> 76.1 us
    pallas_call x1, Pallas kernels: 78.1 us -> 76.1 us  [body(): pl.pallas_call(functools.partial(kernel, n, dp, slots, clips), out_shape=...]
where the time goes in v3:
time: 79.8 us; the launch traced here: 79.6 us
  Pallas kernels  76.1 us (95%)
  local copies, waits for them, and re-layouts  2.85 us (4%)
    pallas_call x1, Pallas kernels, body(): pl.pallas_call(functools.partial(kernel, n, dp, slots, clips), out_shape=...  76.1 us
    unnamed x3, local copies, waits for them, and re-layouts  2.85 us

profile of v3, /device:TPU:0, one launch (start us, length us, event | category | flops | bytes accessed | tf_op | source)
XLA Modules:
  0.0 79.6 jit_solution(1084872562867032178)
XLA Ops:
  0.6 76.1 %shard_map.85 = (bf16[3,128,3072]{2,1,0:T(8,128)(2,1)S(1)}, bf16[128,3072]{1,0:T(8,128)(2,1)S(1)}, f32[2,128]{1,0:T(2,128)S(1)}) custom-call(bf16[3,128,3072]{2,1,0:T(8,128)(2,1)} %bitcast.10, bf16[128,3072]{1,0:T(8,128)(2,1)} %bitcast.11, f32[1,128]{1,0:T(1,128)} %bitcast.14, f32[1,128]{1,0:T(1,128)} %bitcast.15, s32[4,4,24]{2,1,0:T(4,128)} %bitcast.12, ...), custom_call_target="tpu_custom_call" | custom-call | flops 2818572288 | bytes 6291456 | tf_op jit(solution)/shard_map/pallas_call | solution.py:298
  76.8 1.4 %copy.12 = bf16[1,3,128,3072]{3,2,1,0:T(8,128)(2,1)} copy(bf16[1,3,128,3072]{3,2,1,0:T(8,128)(2,1)S(1)} %bitcast.8) | data formatting | bytes 4718592
  78.2 0.9 %copy.13 = bf16[1,128,3072]{2,1,0:T(8,128)(2,1)} copy(bf16[1,128,3072]{2,1,0:T(8,128)(2,1)S(1)} %bitcast.9) | data formatting | bytes 1572864
  79.1 0.6 copy.14

commit v4 on v3

--- a/solution.py
+++ b/solution.py
@@ -139,8 +139,9 @@
             ),
         )
 
+    order = sorted(range(1, n), key=lambda step: abs(2 * step - n))
     barrier = pltpu.get_barrier_semaphore()
-    for step in range(1, n):
+    for step in order:
         pl.semaphore_signal(
             barrier, inc=1, device_id={"head": lax.rem(me + step, n)}, device_id_type=MESH
         )
@@ -149,15 +150,18 @@
         pl.semaphore_signal(
             barrier, inc=1, device_id={"dp": partner(my_dp, bit)}, device_id_type=MESH
         )
-    pl.semaphore_wait(barrier, n - 1 + len(bits))
-
     @pl.loop(0, slots)
     def _(slot):
-        for step in range(1, n):
+        for copy in own_copies(slot):
+            copy.start()
+
+    pl.semaphore_wait(barrier, n - 1 + len(bits))
+
+    @pl.loop(0, slots)
+    def _(slot):
+        for step in order:
             for copy in forward_copies(slot, step, me):
                 copy.start()
-        for copy in own_copies(slot):
-            copy.start()
 
     sums[...] = jnp.zeros_like(sums)
     small_copies = [
@@ -182,7 +186,7 @@
     def _(slot):
         for copy in own_copies(slot):
             copy.wait()
-        for step in range(1, n):
+        for step in order:
             for copy in forward_copies(slot, step, lax.rem(me + n - step, n)):
                 copy.wait_recv()
         head = me * slots + slot
@@ -224,7 +228,7 @@
             raw_grad, gain_part = norm_backward(grad_key, unit, inv, k_gain)
             res_buf[slot, 1, here] = raw_grad
             sums[1:2] += gain_part
-        for step in range(1, n):
+        for step in order:
             for copy in back_copies(slot, step, me):
                 copy.start()
         for copy in own_back_copies(slot):
@@ -271,7 +275,7 @@
 
     @pl.loop(0, slots)
     def _(slot):
-        for step in range(1, n):
+        for step in order:
             for copy in forward_copies(slot, step, me):
                 copy.wait_send()
             for copy in back_copies(slot, step, me):

time: 79.8 us -> 79.8 us (level)
  no operation moved by 1% of the time
where the time goes in v4:
time: 79.8 us; the launch traced here: 79.6 us
  Pallas kernels  76.1 us (95%)
  local copies, waits for them, and re-layouts  2.85 us (4%)
    pallas_call x1, Pallas kernels, body(): pl.pallas_call(functools.partial(kernel, n, dp, slots, clips), out_shape=...  76.1 us
    unnamed x3, local copies, waits for them, and re-layouts  2.85 us

profile of v4, /device:TPU:0, one launch (start us, length us, event | category | flops | bytes accessed | tf_op | source)
XLA Modules:
  0.0 79.6 jit_solution(10350838342094818985)
XLA Ops:
  0.6 76.1 %shard_map.85 = (bf16[3,128,3072]{2,1,0:T(8,128)(2,1)S(1)}, bf16[128,3072]{1,0:T(8,128)(2,1)S(1)}, f32[2,128]{1,0:T(2,128)S(1)}) custom-call(bf16[3,128,3072]{2,1,0:T(8,128)(2,1)} %bitcast.10, bf16[128,3072]{1,0:T(8,128)(2,1)} %bitcast.11, f32[1,128]{1,0:T(1,128)} %bitcast.14, f32[1,128]{1,0:T(1,128)} %bitcast.15, s32[4,4,24]{2,1,0:T(4,128)} %bitcast.12, ...), custom_call_target="tpu_custom_call" | custom-call | flops 2818572288 | bytes 6291456 | tf_op jit(solution)/shard_map/pallas_call | solution.py:302
  76.8 1.4 %copy.12 = bf16[1,3,128,3072]{3,2,1,0:T(8,128)(2,1)} copy(bf16[1,3,128,3072]{3,2,1,0:T(8,128)(2,1)S(1)} %bitcast.8) | data formatting | bytes 4718592
  78.2 0.9 %copy.13 = bf16[1,128,3072]{2,1,0:T(8,128)(2,1)} copy(bf16[1,128,3072]{2,1,0:T(8,128)(2,1)S(1)} %bitcast.9) | data formatting | bytes 1572864
  79.1 0.6 copy.14
